TPU v7x, 128 devices: a whole 4x4x4 slice. The times are simulated.
128 devices in a mesh: dp: 16 (over z, y), sub: 8 (over x, core).
Axes of the slice: x: 4, y: 4, z: 4, core: 2. Of those that a mesh axis runs over, the one named last changes fastest.
Arguments:
- embeddings: bfloat16 [262144, 512], P(('dp', 'sub')), may hold values from -6 to 6
- assignment: int32 [262144, 1], P(('dp', 'sub')), may hold values from 0 to 511; in each aligned block of 2048 rows (0 to 2047, 2048 to 4095, ...) at most 8 rows name the same one
- cluster_order: int32 [512], replicated, may hold values from 0 to 511, each once
Outputs:
- centroids: float32 [512, 512], P(('dp', 'sub'))
- row_max: float32 [262144], P(('dp', 'sub'))
- center_cos: float32 [262144], P(('dp', 'sub'))
Inputs may be any that keep to these rules, and one draw needn't show every extreme that they name: `assignment`: each cluster is named by at most 8 rows of one device (aligned blocks of 2048 rows), and by exactly 8 in some blocks. `cluster_order`: a permutation of the clusters.
All inputs are finite; a program needn't handle non-finite values.
Results may differ from a plain program's by a relative error of at most 0.0029.
Values may be sent and summed in bfloat16 or wider, within the bound.
No kernel may reach another device: no remote copies, remote signals or barrier semaphores. Data moves between devices by JAX's collectives and lax.ppermute only.
A program may use at most 64 MiB of HBM per device.

v0:
```python
import functools

import jax
import jax.numpy as jnp
from jax import lax
from jax.experimental import pallas as pl
from jax.experimental.pallas import tpu as pltpu
from jax.sharding import PartitionSpec as P

F32 = jnp.float32
BF16 = jnp.bfloat16
LANES = 128
EMPTY = 2.0
BARRED = -4.0


def place_kernel(slot_size, step_slots, lab_ref, order_ref, emb_ref, out_ref, flat_ref, unit, order_col, counts):
    rows = emb_ref.shape[0]
    clusters = order_ref.shape[1]
    step = pl.program_id(0)
    width = 256

    @pl.when(step == 0)
    def _():
        @pl.loop(0, rows // width)
        def _(b):
            at = pl.ds(pl.multiple_of(b * width, width), width)
            x = emb_ref[at, :].astype(F32)
            ss = jnp.sum(x * x, axis=1, keepdims=True)
            unit[at, :] = (x * lax.rsqrt(ss + 1e-06)).astype(BF16)

        wide = jnp.broadcast_to(order_ref[...].astype(F32), (LANES, clusters))
        order_col[...] = wide.T.astype(jnp.int32)
        s = lax.broadcasted_iota(jnp.int32, (width, width + LANES), 0)
        r = lax.broadcasted_iota(jnp.int32, (width, width + LANES), 1)
        earlier = jnp.where((s < r) | (r >= width), 1.0, 0.0).astype(BF16)
        base = (lax.broadcasted_iota(jnp.int32, (clusters, LANES), 0) * slot_size).astype(F32)
        counts[...] = jnp.zeros_like(counts)
        for b in range(rows // width):
            lab = lab_ref[:, b * width : (b + 1) * width]
            col = order_col[...]
            eq = [col == lab[:, j * LANES : (j + 1) * LANES] for j in range(width // LANES)]
            hot = jnp.concatenate([jnp.where(e, 1.0, 0.0) for e in eq], axis=1).astype(BF16)
            before = jnp.dot(hot, earlier, preferred_element_type=F32)
            carry = counts[...]
            for j in range(width // LANES):
                val = before[:, j * LANES : (j + 1) * LANES] + (carry + base)
                flat = jnp.sum(jnp.where(eq[j], val, 0.0), axis=0, keepdims=True)
                flat_ref[:, b * width + j * LANES : b * width + (j + 1) * LANES] = flat.astype(jnp.int32)
            counts[...] = carry + before[:, width:]

    here = step * step_slots
    ids = here + lax.broadcasted_iota(jnp.int32, (step_slots, rows), 0)
    hits = jnp.where(ids == flat_ref[...], 1.0, 0.0).astype(BF16)
    placed = jnp.dot(hits, unit[...], preferred_element_type=F32)
    groups = step_slots // slot_size
    have = counts[pl.ds(pl.multiple_of(step * groups, groups), groups), :]
    have = jnp.broadcast_to(have[:, None, :], (groups, slot_size, LANES)).reshape(step_slots, LANES)
    rank = lax.rem(lax.broadcasted_iota(jnp.int32, (step_slots, LANES), 0), slot_size).astype(F32)
    first = jnp.where(rank >= have, EMPTY, placed[:, :LANES])
    out_ref[:, :LANES] = first.astype(BF16)
    out_ref[:, LANES:] = placed[:, LANES:].astype(BF16)


def place(labels, order, embeddings, slot_size):
    rows, feats = embeddings.shape
    clusters = order.shape[1]
    slots = clusters * slot_size
    step_slots = 512
    whole = lambda i: (0, 0)
    return pl.pallas_call(
        functools.partial(place_kernel, slot_size, step_slots),
        grid=(slots // step_slots,),
        in_specs=[
            pl.BlockSpec((1, rows), whole),
            pl.BlockSpec((1, clusters), whole),
            pl.BlockSpec((rows, feats), whole),
        ],
        out_specs=[
            pl.BlockSpec((step_slots, feats), lambda i: (i, 0)),
            pl.BlockSpec((1, rows), whole),
        ],
        out_shape=[
            jax.ShapeDtypeStruct((slots, feats), BF16),
            jax.ShapeDtypeStruct((1, rows), jnp.int32),
        ],
        scratch_shapes=[
            pltpu.VMEM((rows, feats), BF16),
            pltpu.VMEM((clusters, LANES), jnp.int32),
            pltpu.VMEM((clusters, LANES), F32),
        ],
        compiler_params=pltpu.CompilerParams(
            dimension_semantics=("arbitrary",), vmem_limit_bytes=32 * 1024 * 1024
        ),
        name="place",
    )(labels, order, embeddings)


def compare_kernel(members, slot_size, in_ref, cent_ref, val_ref, held, pen, sums):
    step = pl.program_id(0)
    rows, feats = in_ref.shape
    sources = rows // (members * slot_size)
    part = sources * slot_size
    per_member = pen.shape[1]
    x = in_ref[...].astype(F32).reshape(sources, members, slot_size, feats)
    at = pl.ds(pl.multiple_of(step * part, part), part)
    for m in range(members):
        first = x[:, m, :, :LANES]
        rest = x[:, m, :, LANES:]
        empty = first > 1.5
        pen[m, at, :] = jnp.where(empty, BARRED, 0.0).reshape(part, LANES)
        first = jnp.where(empty, 0.0, first)
        held[m, at, :LANES] = first.reshape(part, LANES).astype(BF16)
        held[m, at, LANES:] = rest.reshape(part, feats - LANES).astype(BF16)
        total = jnp.concatenate([jnp.sum(first, axis=0), jnp.sum(rest, axis=0)], axis=1)

        @pl.when(step == 0)
        def _():
            sums[m] = total

        @pl.when(step > 0)
        def _():
            sums[m] += total

    @pl.when(step == pl.num_programs(0) - 1)
    def _():
        for m in range(members):
            s = jnp.sum(sums[m], axis=0, keepdims=True)
            center = s * lax.rsqrt(jnp.sum(s * s, axis=1, keepdims=True) + 1e-06)
            cent_ref[m : m + 1, :] = center
            high = center.astype(BF16).astype(F32)
            row = lax.broadcasted_iota(jnp.int32, (16, feats), 0)
            both = jnp.where(row == 0, high, jnp.where(row == 1, center - high, 0.0))
            held[m, per_member : per_member + 16, :] = both.astype(BF16)
        cols = 256
        for m in range(members):
            for j in range(per_member // cols):
                right = held[m, j * cols : (j + 1) * cols, :]
                gram = lax.dot_general(
                    held[m], right, (((1,), (1,)), ((), ())), preferred_element_type=F32
                )
                cosine = gram[per_member : per_member + 1] + gram[per_member + 1 : per_member + 2]
                val_ref[2 * m + 1 : 2 * m + 2, j * cols : (j + 1) * cols] = cosine
                best = jnp.full((1, cols), -1.0, F32)
                for i in range(per_member // cols):
                    block = gram[i * cols : (i + 1) * cols]
                    barred = pen[m, i * cols : (i + 1) * cols, :]
                    block = block + jnp.concatenate([barred] * (cols // LANES), axis=1)
                    if i == j:
                        a = lax.broadcasted_iota(jnp.int32, (cols, cols), 0)
                        b = lax.broadcasted_iota(jnp.int32, (cols, cols), 1)
                        block = jnp.where(a == b, BARRED, block)
                    best = jnp.maximum(best, jnp.max(block, axis=0, keepdims=True))
                val_ref[2 * m : 2 * m + 1, j * cols : (j + 1) * cols] = best


def compare(arrived, members, slot_size):
    slots, feats = arrived.shape
    per_member = slots // members
    step_rows = 512
    whole = lambda i: (0, 0)
    return pl.pallas_call(
        functools.partial(compare_kernel, members, slot_size),
        grid=(slots // step_rows,),
        in_specs=[pl.BlockSpec((step_rows, feats), lambda i: (i, 0))],
        out_specs=[
            pl.BlockSpec((members, feats), whole),
            pl.BlockSpec((2 * members, per_member), whole),
        ],
        out_shape=[
            jax.ShapeDtypeStruct((members, feats), F32),
            jax.ShapeDtypeStruct((2 * members, per_member), F32),
        ],
        scratch_shapes=[
            pltpu.VMEM((members, per_member + 16, feats), BF16),
            pltpu.VMEM((members, per_member, LANES), F32),
            pltpu.VMEM((members, slot_size, feats), F32),
        ],
        compiler_params=pltpu.CompilerParams(
            dimension_semantics=("arbitrary",), vmem_limit_bytes=32 * 1024 * 1024
        ),
        name="compare",
    )(arrived)


def pick_kernel(members, slot_size, back_ref, flat_ref, max_ref, cos_ref):
    owners = back_ref.shape[0]
    rows = flat_ref.shape[1]
    each = 2 * slot_size
    turned = back_ref[...].T
    wide = jnp.concatenate([turned[m * each : (m + 1) * each] for m in range(members)], axis=1)
    high = wide.astype(BF16)
    left = wide - high.astype(F32)
    mid = left.astype(BF16)
    low = (left - mid.astype(F32)).astype(BF16)
    pieces = jnp.concatenate([high, mid, low], axis=0)
    cols = 512
    owner = lax.broadcasted_iota(jnp.int32, (owners, cols), 0) * members
    for b in range(rows // cols):
        at = slice(b * cols, (b + 1) * cols)
        flat = flat_ref[:, at]
        group = lax.div(flat, slot_size)
        rank = lax.rem(flat, slot_size)
        hits = jnp.concatenate(
            [jnp.where(owner == group - m, 1.0, 0.0).astype(BF16) for m in range(members)], axis=0
        )
        got = jnp.dot(pieces, hits, preferred_element_type=F32)
        got = got[:each] + got[each : 2 * each] + got[2 * each :]
        mine = lax.broadcasted_iota(jnp.int32, (slot_size, cols), 0) == rank
        max_ref[:, at] = jnp.sum(jnp.where(mine, got[:slot_size], 0.0), axis=0, keepdims=True)
        cos_ref[:, at] = jnp.sum(jnp.where(mine, got[slot_size:], 0.0), axis=0, keepdims=True)


def pick(back, flat, members, slot_size):
    rows = flat.shape[1]
    return pl.pallas_call(
        functools.partial(pick_kernel, members, slot_size),
        out_shape=[jax.ShapeDtypeStruct((1, rows), F32)] * 2,
        compiler_params=pltpu.CompilerParams(vmem_limit_bytes=32 * 1024 * 1024),
        name="pick",
    )(back, flat)


def on_device(embeddings, assignment, cluster_order):
    devices = lax.axis_size("dp") * lax.axis_size("sub")
    rows, feats = embeddings.shape
    clusters = cluster_order.shape[0]
    members = clusters // devices
    slot_size = 2 * rows // clusters
    both = ("dp", "sub")
    outgoing, flat = place(
        assignment.reshape(1, rows), cluster_order.reshape(1, clusters), embeddings, slot_size
    )
    arrived = lax.all_to_all(
        outgoing.reshape(devices, members * slot_size, feats), both, split_axis=0, concat_axis=0, tiled=True
    )
    centers, values = compare(arrived.reshape(clusters * slot_size, feats), members, slot_size)
    values = jnp.transpose(values.reshape(2 * members, devices, slot_size), (1, 0, 2))
    back = lax.all_to_all(
        values.reshape(devices, 2 * members * slot_size), both, split_axis=0, concat_axis=0, tiled=True
    )
    row_max, center_cos = pick(back, flat, members, slot_size)
    return centers, row_max.reshape(rows), center_cos.reshape(rows)


def solution(mesh):
    return jax.shard_map(
        on_device,
        mesh=mesh,
        in_specs=(P(("dp", "sub"), None), P(("dp", "sub"), None), P()),
        out_specs=(P(("dp", "sub"), None), P(("dp", "sub")), P(("dp", "sub"))),
        check_vma=False,
    )
```

profile of v0, /device:TPU:1, one launch (start us, length us, event | category | flops | bytes accessed | tf_op | source)
XLA Modules:
  0.0 102.4 jit_solution(16548708792966124955)
XLA Ops:
  0.6 0.0 copy-start
  0.6 1.6 %copy-done = bf16[2048,512]{1,0:T(8,128)(2,1)S(1)} copy-done((bf16[2048,512]{1,0:T(8,128)(2,1)S(1)}, bf16[2048,512]{1,0:T(8,128)(2,1)}, u32[]{:S(2)}) %copy-start) | copy-done | bytes 2097176
  2.2 0.0 copy-start.1
  2.2 0.7 copy-done.1
  2.9 0.0 copy-start.2
  2.9 0.7 copy-done.2
  3.6 12.5 %place.1 = (bf16[4096,512]{1,0:T(8,128)(2,1)S(1)}, s32[1,2048]{1,0:T(1,128)S(1)}) custom-call(s32[1,2048]{1,0:T(1,128)S(1)} %bitcast.12, s32[1,512]{1,0:T(1,128)S(1)} %bitcast.13, bf16[2048,512]{1,0:T(8,128)(2,1)S(1)} %copy-done), custom_call_target="tpu_custom_call" | custom-call | tf_op jit(solution)/shard_map/place/pallas_call | solution.py:71
  16.1 64.3 %all_to_all.16 = bf16[128,32,512]{2,1,0:T(8,128)(2,1)S(1)} all-to-all(bf16[128,32,512]{2,1,0:T(8,128)(2,1)S(1)} %bitcast.10), channel_id=1, replica_groups=mesh['dp'=16,'sub'=8] {'dp','sub'}, dimensions={0} | all-to-all | bytes 8388608 | tf_op jit(solution)/shard_map/all_to_all | solution.py:234
  80.4 6.9 %compare.1 = (f32[4,512]{1,0:T(4,128)}, f32[8,1024]{1,0:T(8,128)S(1)}) custom-call(bf16[4096,512]{1,0:T(8,128)(2,1)S(1)} %bitcast.9), custom_call_target="tpu_custom_call" | custom-call | tf_op jit(solution)/shard_map/compare/pallas_call | solution.py:162
  87.3 0.3 reshape.35
  87.6 0.2 copy.9
  87.8 0.1 copy.10
  87.9 13.5 %all_to_all.17 = f32[128,1,64]{2,1,0:T(1,128)S(1)} all-to-all(f32[128,1,64]{2,1,0:T(1,128)S(1)} %copy.10), channel_id=1, replica_groups=mesh['dp'=16,'sub'=8] {'dp','sub'}, dimensions={0} | all-to-all | bytes 65536 | tf_op jit(solution)/shard_map/all_to_all | solution.py:239
  101.3 1.1 %pick.1 = (f32[1,2048]{1,0:T(1,128)}, f32[1,2048]{1,0:T(1,128)}) custom-call(f32[128,64]{1,0:T(8,128)S(1)} %bitcast.11, s32[1,2048]{1,0:T(1,128)S(1)} %get-tuple-element.12.flat_ref), custom_call_target="tpu_custom_call" | custom-call | tf_op jit(solution)/shard_map/pick/pallas_call | solution.py:216
Async XLA Ops:
  0.6 1.6 %copy-start = (bf16[2048,512]{1,0:T(8,128)(2,1)S(1)}, bf16[2048,512]{1,0:T(8,128)(2,1)}, u32[]{:S(2)}) copy-start(bf16[2048,512]{1,0:T(8,128)(2,1)} %emb_ref.1) | copy-start | bytes 6291460
  2.2 0.7 copy-start.1
  2.9 0.7 copy-start.2
where the time goes:
time: 103 us; the launch traced here: 102 us
  blocking collectives  77.7 us (75%)
  Pallas kernels  20.5 us (20%)
  local copies, waits for them, and re-layouts  3.53 us (3%)
    all_to_all x1, blocking collectives, on_device(): lax.all_to_all(outgoing.reshape(devices, members * slot_size, feats), bot...  64.3 us
    all_to_all x1, blocking collectives, on_device(): lax.all_to_all(values.reshape(devices, 2 * members * slot_size), both, sp...  13.5 us
    pallas_call x1, Pallas kernels, place(): pl.pallas_call(functools.partial(place_kernel, slot_size, step_slots), gr...  12.5 us
    pallas_call x1, Pallas kernels, compare(): pl.pallas_call(functools.partial(compare_kernel, members, slot_size), gri...  6.92 us
    unnamed x6, local copies, waits for them, and re-layouts  2.96 us

commit v1 on v0

v1 whole, which is shorter than its diff:
```python
import functools

import jax
import jax.numpy as jnp
from jax import lax
from jax.experimental import pallas as pl
from jax.experimental.pallas import tpu as pltpu
from jax.sharding import PartitionSpec as P

F32 = jnp.float32
BF16 = jnp.bfloat16
LANES = 128
EMPTY = 2.0
BARRED = -4.0


def place_kernel(slot_size, step_slots, lab_hbm, order_hbm, emb_hbm, out_ref, flat_ref, lab_ref, order_ref, emb_ref, unit, sems):
    rows = emb_ref.shape[0]
    clusters = order_ref.shape[1]
    width = 256
    loads = [
        pltpu.make_async_copy(lab_hbm, lab_ref, sems.at[0]),
        pltpu.make_async_copy(order_hbm, order_ref, sems.at[1]),
        pltpu.make_async_copy(emb_hbm, emb_ref, sems.at[2]),
    ]
    for load in loads:
        load.start()
    s = lax.broadcasted_iota(jnp.int32, (width, width + LANES), 0)
    r = lax.broadcasted_iota(jnp.int32, (width, width + LANES), 1)
    earlier = jnp.where((s < r) | (r >= width), 1.0, 0.0).astype(BF16)
    base = (lax.broadcasted_iota(jnp.int32, (clusters, LANES), 0) * slot_size).astype(F32)
    loads[0].wait()
    loads[1].wait()
    wide = jnp.broadcast_to(order_ref[...].astype(F32), (LANES, clusters))
    col = wide.T.astype(jnp.int32)
    carry = jnp.zeros((clusters, LANES), F32)
    for b in range(rows // width):
        lab = lab_ref[:, b * width : (b + 1) * width]
        eq = [col == lab[:, j * LANES : (j + 1) * LANES] for j in range(width // LANES)]
        hot = jnp.concatenate([jnp.where(e, 1.0, 0.0) for e in eq], axis=1).astype(BF16)
        before = jnp.dot(hot, earlier, preferred_element_type=F32)
        for j in range(width // LANES):
            val = before[:, j * LANES : (j + 1) * LANES] + (carry + base)
            flat = jnp.sum(jnp.where(eq[j], val, 0.0), axis=0, keepdims=True)
            flat_ref[:, b * width + j * LANES : b * width + (j + 1) * LANES] = flat.astype(jnp.int32)
        carry = carry + before[:, width:]
    loads[2].wait()
    groups = step_slots // slot_size
    rank = lax.rem(lax.broadcasted_iota(jnp.int32, (step_slots, LANES), 0), slot_size).astype(F32)
    for b in range(rows // width):
        at = slice(b * width, (b + 1) * width)
        x = emb_ref[at, :].astype(F32)
        ss = jnp.sum(x * x, axis=1, keepdims=True)
        unit[at, :] = (x * lax.rsqrt(ss + 1e-06)).astype(BF16)
    for step in range(out_ref.shape[0] // step_slots):
        here = step * step_slots
        ids = here + lax.broadcasted_iota(jnp.int32, (step_slots, rows), 0)
        hits = jnp.where(ids == flat_ref[...], 1.0, 0.0).astype(BF16)
        placed = jnp.dot(hits, unit[...], preferred_element_type=F32)
        have = carry[step * groups : (step + 1) * groups]
        have = jnp.broadcast_to(have[:, None, :], (groups, slot_size, LANES)).reshape(step_slots, LANES)
        first = jnp.where(rank >= have, EMPTY, placed[:, :LANES])
        out_ref[here : here + step_slots, :LANES] = first.astype(BF16)
        out_ref[here : here + step_slots, LANES:] = placed[:, LANES:].astype(BF16)


def place(labels, order, embeddings, slot_size):
    rows, feats = embeddings.shape
    clusters = order.shape[1]
    slots = clusters * slot_size
    step_slots = 1024
    hbm = pl.BlockSpec(memory_space=pltpu.HBM)
    vmem = pl.BlockSpec(memory_space=pltpu.VMEM)
    return pl.pallas_call(
        functools.partial(place_kernel, slot_size, step_slots),
        in_specs=[hbm, hbm, hbm],
        out_specs=[vmem, vmem],
        out_shape=[
            pltpu.VMEM((slots, feats), BF16),
            pltpu.VMEM((1, rows), jnp.int32),
        ],
        scratch_shapes=[
            pltpu.VMEM((1, rows), jnp.int32),
            pltpu.VMEM((1, clusters), jnp.int32),
            pltpu.VMEM((rows, feats), BF16),
            pltpu.VMEM((rows, feats), BF16),
            pltpu.SemaphoreType.DMA((3,)),
        ],
        compiler_params=pltpu.CompilerParams(vmem_limit_bytes=40 * 1024 * 1024),
        name="place",
    )(*(pltpu.with_memory_space_constraint(v, pltpu.HBM) for v in (labels, order, embeddings)))


def compare_kernel(members, slot_size, in_ref, cent_ref, val_ref, held, pen):
    sources, slots, feats = in_ref.shape
    per_member = pen.shape[1]
    batch = 16
    part = batch * slot_size
    cols = 256
    for pair in range(0, members, 2):
        sums = [None, None]
        for g in range(sources // batch):
            x = in_ref[g * batch : (g + 1) * batch, pair * slot_size : (pair + 2) * slot_size, :].astype(F32)
            for h in range(2):
                m = pair + h
                at = slice(g * part, (g + 1) * part)
                first = x[:, h * slot_size : (h + 1) * slot_size, :LANES]
                rest = x[:, h * slot_size : (h + 1) * slot_size, LANES:]
                empty = first > 1.5
                pen[m, at, :] = jnp.where(empty, BARRED, 0.0).reshape(part, LANES)
                first = jnp.where(empty, 0.0, first)
                held[m, at, :LANES] = first.reshape(part, LANES).astype(BF16)
                held[m, at, LANES:] = rest.reshape(part, feats - LANES).astype(BF16)
                total = jnp.concatenate([jnp.sum(first, axis=0), jnp.sum(rest, axis=0)], axis=1)
                sums[h] = total if g == 0 else sums[h] + total
        for h in range(2):
            m = pair + h
            s = jnp.sum(sums[h], axis=0, keepdims=True)
            center = s * lax.rsqrt(jnp.sum(s * s, axis=1, keepdims=True) + 1e-06)
            cent_ref[m : m + 1, :] = center
            high = center.astype(BF16).astype(F32)
            row = lax.broadcasted_iota(jnp.int32, (16, feats), 0)
            both = jnp.where(row == 0, high, jnp.where(row == 1, center - high, 0.0))
            held[m, per_member : per_member + 16, :] = both.astype(BF16)
            for j in range(per_member // cols):
                right = held[m, j * cols : (j + 1) * cols, :]
                gram = lax.dot_general(
                    held[m], right, (((1,), (1,)), ((), ())), preferred_element_type=F32
                )
                cosine = gram[per_member : per_member + 1] + gram[per_member + 1 : per_member + 2]
                val_ref[2 * m + 1 : 2 * m + 2, j * cols : (j + 1) * cols] = cosine
                best = jnp.full((1, cols), -1.0, F32)
                for i in range(per_member // cols):
                    block = gram[i * cols : (i + 1) * cols]
                    barred = pen[m, i * cols : (i + 1) * cols, :]
                    block = block + jnp.concatenate([barred] * (cols // LANES), axis=1)
                    if i == j:
                        a = lax.broadcasted_iota(jnp.int32, (cols, cols), 0)
                        b = lax.broadcasted_iota(jnp.int32, (cols, cols), 1)
                        block = jnp.where(a == b, BARRED, block)
                    best = jnp.maximum(best, jnp.max(block, axis=0, keepdims=True))
                val_ref[2 * m : 2 * m + 1, j * cols : (j + 1) * cols] = best


def compare(arrived, members, slot_size):
    slots, feats = arrived.shape
    per_member = slots // members
    sources = per_member // slot_size
    vmem = pl.BlockSpec(memory_space=pltpu.VMEM)
    return pl.pallas_call(
        functools.partial(compare_kernel, members, slot_size),
        in_specs=[vmem],
        out_specs=[vmem, vmem],
        out_shape=[
            jax.ShapeDtypeStruct((members, feats), F32),
            jax.ShapeDtypeStruct((2 * members, per_member), F32),
        ],
        scratch_shapes=[
            pltpu.VMEM((members, per_member + 16, feats), BF16),
            pltpu.VMEM((members, per_member, LANES), F32),
        ],
        compiler_params=pltpu.CompilerParams(vmem_limit_bytes=40 * 1024 * 1024),
        name="compare",
    )(pltpu.with_memory_space_constraint(arrived.reshape(sources, members * slot_size, feats), pltpu.VMEM))


def pick_kernel(members, slot_size, back_ref, flat_ref, max_ref, cos_ref):
    owners = back_ref.shape[0]
    rows = flat_ref.shape[1]
    each = 2 * slot_size
    turned = back_ref[...].T
    wide = jnp.concatenate([turned[m * each : (m + 1) * each] for m in range(members)], axis=1)
    high = wide.astype(BF16)
    left = wide - high.astype(F32)
    mid = left.astype(BF16)
    low = (left - mid.astype(F32)).astype(BF16)
    pieces = jnp.concatenate([high, mid, low], axis=0)
    cols = 512
    owner = lax.broadcasted_iota(jnp.int32, (owners, cols), 0) * members
    for b in range(rows // cols):
        at = slice(b * cols, (b + 1) * cols)
        flat = flat_ref[:, at]
        group = lax.div(flat, slot_size)
        rank = lax.rem(flat, slot_size)
        hits = jnp.concatenate(
            [jnp.where(owner == group - m, 1.0, 0.0).astype(BF16) for m in range(members)], axis=0
        )
        got = jnp.dot(pieces, hits, preferred_element_type=F32)
        got = got[:each] + got[each : 2 * each] + got[2 * each :]
        mine = lax.broadcasted_iota(jnp.int32, (slot_size, cols), 0) == rank
        max_ref[:, at] = jnp.sum(jnp.where(mine, got[:slot_size], 0.0), axis=0, keepdims=True)
        cos_ref[:, at] = jnp.sum(jnp.where(mine, got[slot_size:], 0.0), axis=0, keepdims=True)


def pick(back, flat, members, slot_size):
    rows = flat.shape[1]
    return pl.pallas_call(
        functools.partial(pick_kernel, members, slot_size),
        out_shape=[jax.ShapeDtypeStruct((1, rows), F32)] * 2,
        compiler_params=pltpu.CompilerParams(vmem_limit_bytes=32 * 1024 * 1024),
        name="pick",
    )(back, flat)


def on_device(embeddings, assignment, cluster_order):
    devices = lax.axis_size("dp") * lax.axis_size("sub")
    rows, feats = embeddings.shape
    clusters = cluster_order.shape[0]
    members = clusters // devices
    slot_size = 2 * rows // clusters
    both = ("dp", "sub")
    outgoing, flat = place(
        assignment.reshape(1, rows), cluster_order.reshape(1, clusters), embeddings, slot_size
    )
    arrived = lax.all_to_all(
        outgoing.reshape(devices, members * slot_size, feats), both, split_axis=0, concat_axis=0, tiled=True
    )
    centers, values = compare(arrived.reshape(clusters * slot_size, feats), members, slot_size)
    values = jnp.transpose(values.reshape(2 * members, devices, slot_size), (1, 0, 2))
    back = lax.all_to_all(
        values.reshape(devices, 2 * members * slot_size), both, split_axis=0, concat_axis=0, tiled=True
    )
    row_max, center_cos = pick(back, flat, members, slot_size)
    return centers, row_max.reshape(rows), center_cos.reshape(rows)


def solution(mesh):
    return jax.shard_map(
        on_device,
        mesh=mesh,
        in_specs=(P(("dp", "sub"), None), P(("dp", "sub"), None), P()),
        out_specs=(P(("dp", "sub"), None), P(("dp", "sub")), P(("dp", "sub"))),
        check_vma=False,
    )
```

time: 103 us -> 96.6 us (0.938)
  Pallas kernels: 20.5 us -> 17.5 us
  local copies, waits for them, and re-layouts: 3.53 us -> 0.57 us
    pallas_call x2, Pallas kernels: 19.4 us -> 16.4 us  [the longest x1 11 us: place(): pl.pallas_call(functools.partial(place_kernel, slot_size, step_slots), in...]
    unnamed x6 -> x0, local copies, waits for them, and re-layouts: 2.96 us -> none
where the time goes in v1:
time: 96.6 us; the launch traced here: 96.5 us
  blocking collectives  77.7 us (80%)
  Pallas kernels  17.5 us (18%)
    all_to_all x1, blocking collectives, on_device(): lax.all_to_all(outgoing.reshape(devices, members * slot_size, feats), bot...  64.3 us
    all_to_all x1, blocking collectives, on_device(): lax.all_to_all(values.reshape(devices, 2 * members * slot_size), both, sp...  13.4 us
    pallas_call x1, Pallas kernels, place(): pl.pallas_call(functools.partial(place_kernel, slot_size, step_slots), in...  11 us
    pallas_call x1, Pallas kernels, compare(): pl.pallas_call(functools.partial(compare_kernel, members, slot_size), in_...  5.41 us

profile of v1, /device:TPU:1, one launch (start us, length us, event | category | flops | bytes accessed | tf_op | source)
XLA Modules:
  0.0 96.5 jit_solution(6624935595793052860)
XLA Ops:
  0.6 11.0 %place.1 = (bf16[4096,512]{1,0:T(8,128)(2,1)S(1)}, s32[1,2048]{1,0:T(1,128)S(1)}) custom-call(s32[1,2048]{1,0:T(1,128)} %bitcast.12, s32[1,512]{1,0:T(1,128)} %bitcast.13, bf16[2048,512]{1,0:T(8,128)(2,1)} %emb_hbm.1), custom_call_target="tpu_custom_call" | custom-call | tf_op jit(solution)/shard_map/place/pallas_call | solution.py:74
  11.6 64.3 %all_to_all.16.in_ref = bf16[128,32,512]{2,1,0:T(8,128)(2,1)S(1)} all-to-all(bf16[128,32,512]{2,1,0:T(8,128)(2,1)S(1)} %bitcast.8), channel_id=1, replica_groups=mesh['dp'=16,'sub'=8] {'dp','sub'}, dimensions={0} | all-to-all | bytes 8388608 | tf_op jit(solution)/shard_map/all_to_all | solution.py:215
  75.9 5.4 %compare.1 = (f32[4,512]{1,0:T(4,128)}, f32[8,1024]{1,0:T(8,128)S(1)}) custom-call(bf16[128,32,512]{2,1,0:T(8,128)(2,1)S(1)} %all_to_all.16.in_ref), custom_call_target="tpu_custom_call" | custom-call | tf_op jit(solution)/shard_map/compare/pallas_call | solution.py:150
  81.3 0.3 reshape.31
  81.6 0.2 copy.9
  81.8 0.1 copy.10
  81.9 13.4 %all_to_all.17 = f32[128,1,64]{2,1,0:T(1,128)S(1)} all-to-all(f32[128,1,64]{2,1,0:T(1,128)S(1)} %copy.10), channel_id=1, replica_groups=mesh['dp'=16,'sub'=8] {'dp','sub'}, dimensions={0} | all-to-all | bytes 65536 | tf_op jit(solution)/shard_map/all_to_all | solution.py:220
  95.3 1.1 %pick.1 = (f32[1,2048]{1,0:T(1,128)}, f32[1,2048]{1,0:T(1,128)}) custom-call(f32[128,64]{1,0:T(8,128)S(1)} %bitcast.9, s32[1,2048]{1,0:T(1,128)S(1)} %get-tuple-element.12.flat_ref), custom_call_target="tpu_custom_call" | custom-call | tf_op jit(solution)/shard_map/pick/pallas_call | solution.py:197

commit v2 on v1

--- a/solution.py
+++ b/solution.py
@@ -122,23 +122,38 @@
             row = lax.broadcasted_iota(jnp.int32, (16, feats), 0)
             both = jnp.where(row == 0, high, jnp.where(row == 1, center - high, 0.0))
             held[m, per_member : per_member + 16, :] = both.astype(BF16)
-            for j in range(per_member // cols):
+            blocks = per_member // cols
+            lane = lax.broadcasted_iota(jnp.int32, (16, LANES), 1)
+            pick_lane = jnp.where(lane == 0, 1.0, 0.0).astype(BF16)
+            barred_cols = lax.dot_general(
+                pick_lane, pen[m].astype(BF16), (((1,), (1,)), ((), ())), preferred_element_type=F32
+            )[:1]
+            across = [None] * blocks
+            for j in range(blocks):
                 right = held[m, j * cols : (j + 1) * cols, :]
                 gram = lax.dot_general(
-                    held[m], right, (((1,), (1,)), ((), ())), preferred_element_type=F32
+                    held[m, j * cols :, :], right, (((1,), (1,)), ((), ())), preferred_element_type=F32
                 )
-                cosine = gram[per_member : per_member + 1] + gram[per_member + 1 : per_member + 2]
+                end = per_member - j * cols
+                cosine = gram[end : end + 1] + gram[end + 1 : end + 2]
                 val_ref[2 * m + 1 : 2 * m + 2, j * cols : (j + 1) * cols] = cosine
                 best = jnp.full((1, cols), -1.0, F32)
-                for i in range(per_member // cols):
-                    block = gram[i * cols : (i + 1) * cols]
+                for i in range(j, blocks):
+                    block = gram[(i - j) * cols : (i - j + 1) * cols]
                     barred = pen[m, i * cols : (i + 1) * cols, :]
-                    block = block + jnp.concatenate([barred] * (cols // LANES), axis=1)
+                    down = block + jnp.concatenate([barred] * (cols // LANES), axis=1)
                     if i == j:
                         a = lax.broadcasted_iota(jnp.int32, (cols, cols), 0)
                         b = lax.broadcasted_iota(jnp.int32, (cols, cols), 1)
-                        block = jnp.where(a == b, BARRED, block)
-                    best = jnp.maximum(best, jnp.max(block, axis=0, keepdims=True))
+                        down = jnp.where(a == b, BARRED, down)
+                    best = jnp.maximum(best, jnp.max(down, axis=0, keepdims=True))
+                    if i > j:
+                        side = block + barred_cols[:, j * cols : (j + 1) * cols]
+                        for k in range(cols // LANES):
+                            piece = side[:, k * LANES : (k + 1) * LANES]
+                            across[i] = piece if across[i] is None else jnp.maximum(across[i], piece)
+                if across[j] is not None:
+                    best = jnp.maximum(best, jnp.max(across[j].T, axis=0, keepdims=True))
                 val_ref[2 * m : 2 * m + 1, j * cols : (j + 1) * cols] = best
 
 

time: 96.6 us -> 95.8 us (level)
  no operation moved by 1% of the time
where the time goes in v2:
time: 95.8 us; the launch traced here: 95.6 us
  blocking collectives  77.7 us (81%)
  Pallas kernels  16.7 us (17%)
    all_to_all x1, blocking collectives, on_device(): lax.all_to_all(outgoing.reshape(devices, members * slot_size, feats), bot...  64.3 us
    all_to_all x1, blocking collectives, on_device(): lax.all_to_all(values.reshape(devices, 2 * members * slot_size), both, sp...  13.4 us
    pallas_call x1, Pallas kernels, place(): pl.pallas_call(functools.partial(place_kernel, slot_size, step_slots), in...  11 us
    pallas_call x1, Pallas kernels, compare(): pl.pallas_call(functools.partial(compare_kernel, members, slot_size), in_...  4.58 us

profile of v2, /device:TPU:1, one launch (start us, length us, event | category | flops | bytes accessed | tf_op | source)
XLA Modules:
  0.0 95.6 jit_solution(6379454169763124178)
XLA Ops:
  0.6 11.0 %place.1 = (bf16[4096,512]{1,0:T(8,128)(2,1)S(1)}, s32[1,2048]{1,0:T(1,128)S(1)}) custom-call(s32[1,2048]{1,0:T(1,128)} %bitcast.12, s32[1,512]{1,0:T(1,128)} %bitcast.13, bf16[2048,512]{1,0:T(8,128)(2,1)} %emb_hbm.1), custom_call_target="tpu_custom_call" | custom-call | tf_op jit(solution)/shard_map/place/pallas_call | solution.py:74
  11.6 64.3 %all_to_all.16.in_ref = bf16[128,32,512]{2,1,0:T(8,128)(2,1)S(1)} all-to-all(bf16[128,32,512]{2,1,0:T(8,128)(2,1)S(1)} %bitcast.8), channel_id=1, replica_groups=mesh['dp'=16,'sub'=8] {'dp','sub'}, dimensions={0} | all-to-all | bytes 8388608 | tf_op jit(solution)/shard_map/all_to_all | solution.py:230
  75.9 4.6 %compare.1 = (f32[4,512]{1,0:T(4,128)}, f32[8,1024]{1,0:T(8,128)S(1)}) custom-call(bf16[128,32,512]{2,1,0:T(8,128)(2,1)S(1)} %all_to_all.16.in_ref), custom_call_target="tpu_custom_call" | custom-call | tf_op jit(solution)/shard_map/compare/pallas_call | solution.py:165
  80.5 0.3 reshape.31
  80.8 0.2 copy.9
  81.0 0.1 copy.10
  81.1 13.4 %all_to_all.17 = f32[128,1,64]{2,1,0:T(1,128)S(1)} all-to-all(f32[128,1,64]{2,1,0:T(1,128)S(1)} %copy.10), channel_id=1, replica_groups=mesh['dp'=16,'sub'=8] {'dp','sub'}, dimensions={0} | all-to-all | bytes 65536 | tf_op jit(solution)/shard_map/all_to_all | solution.py:235
  94.5 1.1 %pick.1 = (f32[1,2048]{1,0:T(1,128)}, f32[1,2048]{1,0:T(1,128)}) custom-call(f32[128,64]{1,0:T(8,128)S(1)} %bitcast.9, s32[1,2048]{1,0:T(1,128)S(1)} %get-tuple-element.12.flat_ref), custom_call_target="tpu_custom_call" | custom-call | tf_op jit(solution)/shard_map/pick/pallas_call | solution.py:212

commit v3 on v2

--- a/solution.py
+++ b/solution.py
@@ -14,10 +14,29 @@
 BARRED = -4.0
 
 
-def place_kernel(slot_size, step_slots, lab_hbm, order_hbm, emb_hbm, out_ref, flat_ref, lab_ref, order_ref, emb_ref, unit, sems):
-    rows = emb_ref.shape[0]
+def place_kernel(
+    slot_size,
+    lab_hbm,
+    order_hbm,
+    emb_hbm,
+    out_ref,
+    flat_ref,
+    lab_ref,
+    order_ref,
+    emb_ref,
+    unit,
+    grouped,
+    plan_vec,
+    plan,
+    sems,
+):
+    rows, feats = emb_ref.shape
     clusters = order_ref.shape[1]
     width = 256
+    blocks = rows // width
+    parts = grouped.shape[0]
+    step_slots = out_ref.shape[0] // parts
+    window = step_slots // parts
     loads = [
         pltpu.make_async_copy(lab_hbm, lab_ref, sems.at[0]),
         pltpu.make_async_copy(order_hbm, order_ref, sems.at[1]),
@@ -25,6 +44,7 @@
     ]
     for load in loads:
         load.start()
+    grouped[...] = jnp.zeros_like(grouped)
     s = lax.broadcasted_iota(jnp.int32, (width, width + LANES), 0)
     r = lax.broadcasted_iota(jnp.int32, (width, width + LANES), 1)
     earlier = jnp.where((s < r) | (r >= width), 1.0, 0.0).astype(BF16)
@@ -34,7 +54,7 @@
     wide = jnp.broadcast_to(order_ref[...].astype(F32), (LANES, clusters))
     col = wide.T.astype(jnp.int32)
     carry = jnp.zeros((clusters, LANES), F32)
-    for b in range(rows // width):
+    for b in range(blocks):
         lab = lab_ref[:, b * width : (b + 1) * width]
         eq = [col == lab[:, j * LANES : (j + 1) * LANES] for j in range(width // LANES)]
         hot = jnp.concatenate([jnp.where(e, 1.0, 0.0) for e in eq], axis=1).astype(BF16)
@@ -44,35 +64,95 @@
             flat = jnp.sum(jnp.where(eq[j], val, 0.0), axis=0, keepdims=True)
             flat_ref[:, b * width + j * LANES : b * width + (j + 1) * LANES] = flat.astype(jnp.int32)
         carry = carry + before[:, width:]
+
+    flat_row = flat_ref[...]
+    part_row = lax.div(flat_row, step_slots)
+    local_row = flat_row - part_row * step_slots
+    part_id = lax.broadcasted_iota(jnp.int32, (parts, width), 0)
+    inside = [part_id == part_row[:, b * width : (b + 1) * width] for b in range(blocks)]
+    hot = jnp.concatenate([jnp.where(e, 1.0, 0.0) for e in inside], axis=0).astype(BF16)
+    before = jnp.dot(hot, earlier, preferred_element_type=F32)
+    lane = lax.broadcasted_iota(jnp.int32, (parts, LANES), 1)
+    start = jnp.zeros((parts, LANES), jnp.int32)
+    most = jnp.zeros((parts, LANES), jnp.int32)
+    table = jnp.zeros((parts, LANES), jnp.int32)
+    target = []
+    for b in range(blocks):
+        mine = before[b * parts : (b + 1) * parts]
+        within = jnp.sum(jnp.where(inside[b], mine[:, :width], 0.0), axis=0, keepdims=True)
+        target.append(part_row[:, b * width : (b + 1) * width] * window + within.astype(jnp.int32))
+        amount = mine[:, width:].astype(jnp.int32)
+        table = jnp.where(lane == b, start, table)
+        most = jnp.maximum(most, amount)
+        start = start + ((amount + 15) & -16)
+    too_far = jnp.max(jnp.where((start > step_slots) | (most > window), 1.0, 0.0), axis=0, keepdims=True)
+    table = jnp.where(lane == blocks, jnp.broadcast_to(too_far, (parts, LANES)).astype(jnp.int32), table)
+    plan_vec[...] = table
+    to_scalars = pltpu.make_async_copy(plan_vec, plan, sems.at[3])
+    to_scalars.start()
+
+    upper = lax.broadcasted_iota(jnp.int32, (LANES, width), 0) < LANES // 2
+    for b in range(blocks):
+        local = local_row[:, b * width : (b + 1) * width]
+        group = lax.div(local, slot_size)
+        both = jnp.where(upper, group, local - group * slot_size).astype(F32)
+        unit[b * width : (b + 1) * width, feats:] = both.T.astype(BF16)
     loads[2].wait()
-    groups = step_slots // slot_size
-    rank = lax.rem(lax.broadcasted_iota(jnp.int32, (step_slots, LANES), 0), slot_size).astype(F32)
-    for b in range(rows // width):
+    for b in range(blocks):
         at = slice(b * width, (b + 1) * width)
         x = emb_ref[at, :].astype(F32)
         ss = jnp.sum(x * x, axis=1, keepdims=True)
-        unit[at, :] = (x * lax.rsqrt(ss + 1e-06)).astype(BF16)
-    for step in range(out_ref.shape[0] // step_slots):
-        here = step * step_slots
-        ids = here + lax.broadcasted_iota(jnp.int32, (step_slots, rows), 0)
-        hits = jnp.where(ids == flat_ref[...], 1.0, 0.0).astype(BF16)
-        placed = jnp.dot(hits, unit[...], preferred_element_type=F32)
-        have = carry[step * groups : (step + 1) * groups]
+        unit[at, :feats] = (x * lax.rsqrt(ss + 1e-06)).astype(BF16)
+    to_scalars.wait()
+    dense = plan[0, blocks]
+
+    groups = step_slots // slot_size
+    rank = lax.rem(lax.broadcasted_iota(jnp.int32, (step_slots, LANES), 0), slot_size).astype(F32)
+
+    def store(part, placed):
+        have = carry[part * groups : (part + 1) * groups]
         have = jnp.broadcast_to(have[:, None, :], (groups, slot_size, LANES)).reshape(step_slots, LANES)
         first = jnp.where(rank >= have, EMPTY, placed[:, :LANES])
-        out_ref[here : here + step_slots, :LANES] = first.astype(BF16)
-        out_ref[here : here + step_slots, LANES:] = placed[:, LANES:].astype(BF16)
+        at = slice(part * step_slots, (part + 1) * step_slots)
+        out_ref[at, :LANES] = first.astype(BF16)
+        out_ref[at, LANES:] = placed[:, LANES:].astype(BF16)
+
+    @pl.when(dense == 0)
+    def _():
+        ids = lax.broadcasted_iota(jnp.int32, (step_slots, width), 0)
+        for b in range(blocks):
+            hits = jnp.where(ids == target[b], 1.0, 0.0).astype(BF16)
+            sorted_rows = jnp.dot(
+                hits, unit[b * width : (b + 1) * width, :], preferred_element_type=F32
+            ).astype(BF16)
+            for part in range(parts):
+                at = pl.ds(pl.multiple_of(plan[part, b], 16), window)
+                grouped[part, at, :] = sorted_rows[part * window : (part + 1) * window]
+        ids = lax.broadcasted_iota(jnp.int32, (step_slots, step_slots), 0)
+        for part in range(parts):
+            turned = grouped[part, :step_slots, feats:].astype(F32).T
+            slot = (turned[:1] * slot_size + turned[LANES // 2 : LANES // 2 + 1]).astype(jnp.int32)
+            hits = jnp.where(ids == slot, 1.0, 0.0).astype(BF16)
+            store(part, jnp.dot(hits, grouped[part, :step_slots, :feats], preferred_element_type=F32))
+
+    @pl.when(dense != 0)
+    def _():
+        ids = lax.broadcasted_iota(jnp.int32, (step_slots, rows), 0)
+        for part in range(parts):
+            hits = jnp.where(ids == flat_ref[...] - part * step_slots, 1.0, 0.0).astype(BF16)
+            store(part, jnp.dot(hits, unit[:, :feats], preferred_element_type=F32))
 
 
 def place(labels, order, embeddings, slot_size):
     rows, feats = embeddings.shape
     clusters = order.shape[1]
     slots = clusters * slot_size
-    step_slots = 1024
+    parts = 8
+    step_slots = slots // parts
     hbm = pl.BlockSpec(memory_space=pltpu.HBM)
     vmem = pl.BlockSpec(memory_space=pltpu.VMEM)
     return pl.pallas_call(
-        functools.partial(place_kernel, slot_size, step_slots),
+        functools.partial(place_kernel, slot_size),
         in_specs=[hbm, hbm, hbm],
         out_specs=[vmem, vmem],
         out_shape=[
@@ -83,10 +163,13 @@
             pltpu.VMEM((1, rows), jnp.int32),
             pltpu.VMEM((1, clusters), jnp.int32),
             pltpu.VMEM((rows, feats), BF16),
-            pltpu.VMEM((rows, feats), BF16),
-            pltpu.SemaphoreType.DMA((3,)),
+            pltpu.VMEM((rows, feats + LANES), BF16),
+            pltpu.VMEM((parts, step_slots + step_slots // parts, feats + LANES), BF16),
+            pltpu.VMEM((parts, LANES), jnp.int32),
+            pltpu.SMEM((parts, LANES), jnp.int32),
+            pltpu.SemaphoreType.DMA((4,)),
         ],
-        compiler_params=pltpu.CompilerParams(vmem_limit_bytes=40 * 1024 * 1024),
+        compiler_params=pltpu.CompilerParams(vmem_limit_bytes=44 * 1024 * 1024),
         name="place",
     )(*(pltpu.with_memory_space_constraint(v, pltpu.HBM) for v in (labels, order, embeddings)))
 

time: 95.8 us -> 92.2 us (0.962)
  Pallas kernels: 16.7 us -> 13.1 us
    pallas_call x1, Pallas kernels: 11 us -> 7.39 us  [place(): pl.pallas_call(functools.partial(place_kernel, slot_size), in_specs=[hbm,...]
where the time goes in v3:
time: 92.2 us; the launch traced here: 92 us
  blocking collectives  77.7 us (84%)
  Pallas kernels  13.1 us (14%)
    all_to_all x1, blocking collectives, on_device(): lax.all_to_all(outgoing.reshape(devices, members * slot_size, feats), bot...  64.3 us
    all_to_all x1, blocking collectives, on_device(): lax.all_to_all(values.reshape(devices, 2 * members * slot_size), both, sp...  13.4 us
    pallas_call x1, Pallas kernels, place(): pl.pallas_call(functools.partial(place_kernel, slot_size), in_specs=[hbm,...  7.39 us
    pallas_call x1, Pallas kernels, compare(): pl.pallas_call(functools.partial(compare_kernel, members, slot_size), in_...  4.58 us

profile of v3, /device:TPU:1, one launch (start us, length us, event | category | flops | bytes accessed | tf_op | source)
XLA Modules:
  0.0 92.0 jit_solution(9391294368731751137)
XLA Ops:
  0.6 7.4 %place.1 = (bf16[4096,512]{1,0:T(8,128)(2,1)S(1)}, s32[1,2048]{1,0:T(1,128)S(1)}) custom-call(s32[1,2048]{1,0:T(1,128)} %bitcast.12, s32[1,512]{1,0:T(1,128)} %bitcast.13, bf16[2048,512]{1,0:T(8,128)(2,1)} %emb_hbm.1), custom_call_target="tpu_custom_call" | custom-call | tf_op jit(solution)/shard_map/place/pallas_call | solution.py:154
  8.0 64.3 %all_to_all.16.in_ref = bf16[128,32,512]{2,1,0:T(8,128)(2,1)S(1)} all-to-all(bf16[128,32,512]{2,1,0:T(8,128)(2,1)S(1)} %bitcast.8), channel_id=1, replica_groups=mesh['dp'=16,'sub'=8] {'dp','sub'}, dimensions={0} | all-to-all | bytes 8388608 | tf_op jit(solution)/shard_map/all_to_all | solution.py:313
  72.3 4.6 %compare.1 = (f32[4,512]{1,0:T(4,128)}, f32[8,1024]{1,0:T(8,128)S(1)}) custom-call(bf16[128,32,512]{2,1,0:T(8,128)(2,1)S(1)} %all_to_all.16.in_ref), custom_call_target="tpu_custom_call" | custom-call | tf_op jit(solution)/shard_map/compare/pallas_call | solution.py:248
  76.9 0.3 reshape.31
  77.2 0.2 copy.9
  77.4 0.1 copy.10
  77.5 13.4 %all_to_all.17 = f32[128,1,64]{2,1,0:T(1,128)S(1)} all-to-all(f32[128,1,64]{2,1,0:T(1,128)S(1)} %copy.10), channel_id=1, replica_groups=mesh['dp'=16,'sub'=8] {'dp','sub'}, dimensions={0} | all-to-all | bytes 65536 | tf_op jit(solution)/shard_map/all_to_all | solution.py:318
  90.9 1.1 %pick.1 = (f32[1,2048]{1,0:T(1,128)}, f32[1,2048]{1,0:T(1,128)}) custom-call(f32[128,64]{1,0:T(8,128)S(1)} %bitcast.9, s32[1,2048]{1,0:T(1,128)S(1)} %get-tuple-element.12.flat_ref), custom_call_target="tpu_custom_call" | custom-call | tf_op jit(solution)/shard_map/pick/pallas_call | solution.py:295

commit v4 on v3

--- a/solution.py
+++ b/solution.py
@@ -174,7 +174,7 @@
     )(*(pltpu.with_memory_space_constraint(v, pltpu.HBM) for v in (labels, order, embeddings)))
 
 
-def compare_kernel(members, slot_size, in_ref, cent_ref, val_ref, held, pen):
+def compare_kernel(members, slot_size, in_ref, cent_ref, back_ref, held, pen, val_ref, turned):
     sources, slots, feats = in_ref.shape
     per_member = pen.shape[1]
     batch = 16
@@ -239,6 +239,25 @@
                     best = jnp.maximum(best, jnp.max(across[j].T, axis=0, keepdims=True))
                 val_ref[2 * m : 2 * m + 1, j * cols : (j + 1) * cols] = best
 
+    values = 2 * members
+    tiles = per_member // LANES
+    stacked = [val_ref[:, i * LANES : (i + 1) * LANES] for i in range(tiles)]
+    turned[...] = jnp.concatenate(stacked + [jnp.zeros((LANES - tiles * values, LANES), F32)], axis=0).T
+    span = LANES // slot_size
+    held_rows = [turned[pl.ds(k, span, stride=slot_size), :] for k in range(slot_size)]
+    group = lax.broadcasted_iota(jnp.int32, (span, LANES), 1) // values
+    bit = 1
+    while bit < slot_size:
+        odd = (group & bit) != 0
+        for k in range(slot_size):
+            if not k & bit:
+                low, high = held_rows[k], held_rows[k | bit]
+                held_rows[k] = jnp.where(odd, pltpu.roll(high, bit * values, axis=1), low)
+                held_rows[k | bit] = jnp.where(odd, high, pltpu.roll(low, LANES - bit * values, axis=1))
+        bit *= 2
+    for i in range(tiles):
+        back_ref[i * span : (i + 1) * span, :] = held_rows[i]
+
 
 def compare(arrived, members, slot_size):
     slots, feats = arrived.shape
@@ -251,23 +270,33 @@
         out_specs=[vmem, vmem],
         out_shape=[
             jax.ShapeDtypeStruct((members, feats), F32),
-            jax.ShapeDtypeStruct((2 * members, per_member), F32),
+            pltpu.VMEM((sources, LANES), F32),
         ],
         scratch_shapes=[
             pltpu.VMEM((members, per_member + 16, feats), BF16),
             pltpu.VMEM((members, per_member, LANES), F32),
+            pltpu.VMEM((2 * members, per_member), F32),
+            pltpu.VMEM((LANES, LANES), F32),
         ],
         compiler_params=pltpu.CompilerParams(vmem_limit_bytes=40 * 1024 * 1024),
         name="compare",
     )(pltpu.with_memory_space_constraint(arrived.reshape(sources, members * slot_size, feats), pltpu.VMEM))
 
 
-def pick_kernel(members, slot_size, back_ref, flat_ref, max_ref, cos_ref):
+def pick_kernel(members, slot_size, back_ref, flat_ref, max_ref, cos_ref, turned):
     owners = back_ref.shape[0]
     rows = flat_ref.shape[1]
     each = 2 * slot_size
-    turned = back_ref[...].T
-    wide = jnp.concatenate([turned[m * each : (m + 1) * each] for m in range(members)], axis=1)
+    turned[...] = back_ref[...].T
+    wide = jnp.concatenate(
+        [
+            jnp.concatenate(
+                [turned[pl.ds(2 * m + v, slot_size, stride=2 * members), :] for v in range(2)], axis=0
+            )
+            for m in range(members)
+        ],
+        axis=1,
+    )
     high = wide.astype(BF16)
     left = wide - high.astype(F32)
     mid = left.astype(BF16)
@@ -295,6 +324,7 @@
     return pl.pallas_call(
         functools.partial(pick_kernel, members, slot_size),
         out_shape=[jax.ShapeDtypeStruct((1, rows), F32)] * 2,
+        scratch_shapes=[pltpu.VMEM((back.shape[1], back.shape[0]), F32)],
         compiler_params=pltpu.CompilerParams(vmem_limit_bytes=32 * 1024 * 1024),
         name="pick",
     )(back, flat)
@@ -314,10 +344,9 @@
         outgoing.reshape(devices, members * slot_size, feats), both, split_axis=0, concat_axis=0, tiled=True
     )
     centers, values = compare(arrived.reshape(clusters * slot_size, feats), members, slot_size)
-    values = jnp.transpose(values.reshape(2 * members, devices, slot_size), (1, 0, 2))
     back = lax.all_to_all(
-        values.reshape(devices, 2 * members * slot_size), both, split_axis=0, concat_axis=0, tiled=True
-    )
+        values.reshape(devices, 1, values.shape[1]), both, split_axis=0, concat_axis=0, tiled=True
+    ).reshape(values.shape)
     row_max, center_cos = pick(back, flat, members, slot_size)
     return centers, row_max.reshape(rows), center_cos.reshape(rows)
 

time: 92.2 us -> 91.8 us (level)
  no operation moved by 1% of the time
where the time goes in v4:
time: 91.8 us; the launch traced here: 91.6 us
  blocking collectives  77.7 us (85%)
  Pallas kernels  13.2 us (14%)
    all_to_all x1, blocking collectives, on_device(): lax.all_to_all(outgoing.reshape(devices, members * slot_size, feats), bot...  64.3 us
    all_to_all x1, blocking collectives, on_device(): lax.all_to_all(values.reshape(devices, 1, values.shape[1]), both, split_a...  13.4 us
    pallas_call x1, Pallas kernels, place(): pl.pallas_call(functools.partial(place_kernel, slot_size), in_specs=[hbm,...  7.39 us
    pallas_call x1, Pallas kernels, compare(): pl.pallas_call(functools.partial(compare_kernel, members, slot_size), in_...  4.69 us

profile of v4, /device:TPU:1, one launch (start us, length us, event | category | flops | bytes accessed | tf_op | source)
XLA Modules:
  0.0 91.6 jit_solution(8838601369467595288)
XLA Ops:
  0.6 7.4 %place.1 = (bf16[4096,512]{1,0:T(8,128)(2,1)S(1)}, s32[1,2048]{1,0:T(1,128)S(1)}) custom-call(s32[1,2048]{1,0:T(1,128)} %bitcast.12, s32[1,512]{1,0:T(1,128)} %bitcast.13, bf16[2048,512]{1,0:T(8,128)(2,1)} %emb_hbm.1), custom_call_target="tpu_custom_call" | custom-call | tf_op jit(solution)/shard_map/place/pallas_call | solution.py:154
  8.0 64.3 %all_to_all.10.in_ref = bf16[128,32,512]{2,1,0:T(8,128)(2,1)S(1)} all-to-all(bf16[128,32,512]{2,1,0:T(8,128)(2,1)S(1)} %bitcast.9), channel_id=1, replica_groups=mesh['dp'=16,'sub'=8] {'dp','sub'}, dimensions={0} | all-to-all | bytes 8388608 | tf_op jit(solution)/shard_map/all_to_all | solution.py:343
  72.3 4.7 %compare.1 = (f32[4,512]{1,0:T(4,128)}, f32[128,128]{1,0:T(8,128)S(1)}) custom-call(bf16[128,32,512]{2,1,0:T(8,128)(2,1)S(1)} %all_to_all.10.in_ref), custom_call_target="tpu_custom_call" | custom-call | tf_op jit(solution)/shard_map/compare/pallas_call | solution.py:267
  77.0 13.4 %all_to_all.11 = f32[128,1,128]{2,1,0:T(1,128)S(1)} all-to-all(f32[128,1,128]{2,1,0:T(1,128)S(1)} %bitcast.11), channel_id=1, replica_groups=mesh['dp'=16,'sub'=8] {'dp','sub'}, dimensions={0} | all-to-all | bytes 131072 | tf_op jit(solution)/shard_map/all_to_all | solution.py:347
  90.5 1.1 %pick.1 = (f32[1,2048]{1,0:T(1,128)}, f32[1,2048]{1,0:T(1,128)}) custom-call(f32[128,128]{1,0:T(8,128)S(1)} %bitcast.10, s32[1,2048]{1,0:T(1,128)S(1)} %get-tuple-element.12.flat_ref), custom_call_target="tpu_custom_call" | custom-call | tf_op jit(solution)/shard_map/pick/pallas_call | solution.py:324

commit v5 on v4

--- a/solution.py
+++ b/solution.py
@@ -103,6 +103,14 @@
         x = emb_ref[at, :].astype(F32)
         ss = jnp.sum(x * x, axis=1, keepdims=True)
         unit[at, :feats] = (x * lax.rsqrt(ss + 1e-06)).astype(BF16)
+    block_ids = lax.broadcasted_iota(jnp.int32, (step_slots, width), 0)
+
+    def sort_block(b):
+        hits = jnp.where(block_ids == target[b], 1.0, 0.0).astype(BF16)
+        rows_of = unit[b * width : (b + 1) * width, :]
+        return jnp.dot(hits, rows_of, preferred_element_type=F32).astype(BF16)
+
+    early = [sort_block(b) for b in range(4)]
     to_scalars.wait()
     dense = plan[0, blocks]
 
@@ -119,12 +127,8 @@
 
     @pl.when(dense == 0)
     def _():
-        ids = lax.broadcasted_iota(jnp.int32, (step_slots, width), 0)
         for b in range(blocks):
-            hits = jnp.where(ids == target[b], 1.0, 0.0).astype(BF16)
-            sorted_rows = jnp.dot(
-                hits, unit[b * width : (b + 1) * width, :], preferred_element_type=F32
-            ).astype(BF16)
+            sorted_rows = early[b] if b < len(early) else sort_block(b)
             for part in range(parts):
                 at = pl.ds(pl.multiple_of(plan[part, b], 16), window)
                 grouped[part, at, :] = sorted_rows[part * window : (part + 1) * window]
@@ -177,7 +181,7 @@
 def compare_kernel(members, slot_size, in_ref, cent_ref, back_ref, held, pen, val_ref, turned):
     sources, slots, feats = in_ref.shape
     per_member = pen.shape[1]
-    batch = 16
+    batch = 8
     part = batch * slot_size
     cols = 256
     for pair in range(0, members, 2):

time: 91.8 us -> 91.6 us (level)
  no operation moved by 1% of the time
where the time goes in v5:
time: 91.6 us; the launch traced here: 91.5 us
  blocking collectives  77.7 us (85%)
  Pallas kernels  13.1 us (14%)
    all_to_all x1, blocking collectives, on_device(): lax.all_to_all(outgoing.reshape(devices, members * slot_size, feats), bot...  64.3 us
    all_to_all x1, blocking collectives, on_device(): lax.all_to_all(values.reshape(devices, 1, values.shape[1]), both, split_a...  13.4 us
    pallas_call x1, Pallas kernels, place(): pl.pallas_call(functools.partial(place_kernel, slot_size), in_specs=[hbm,...  7.28 us
    pallas_call x1, Pallas kernels, compare(): pl.pallas_call(functools.partial(compare_kernel, members, slot_size), in_...  4.66 us

profile of v5, /device:TPU:1, one launch (start us, length us, event | category | flops | bytes accessed | tf_op | source)
XLA Modules:
  0.0 91.5 jit_solution(341111480675295373)
XLA Ops:
  0.6 7.3 %place.1 = (bf16[4096,512]{1,0:T(8,128)(2,1)S(1)}, s32[1,2048]{1,0:T(1,128)S(1)}) custom-call(s32[1,2048]{1,0:T(1,128)} %bitcast.12, s32[1,512]{1,0:T(1,128)} %bitcast.13, bf16[2048,512]{1,0:T(8,128)(2,1)} %emb_hbm.1), custom_call_target="tpu_custom_call" | custom-call | tf_op jit(solution)/shard_map/place/pallas_call | solution.py:158
  7.9 64.3 %all_to_all.10.in_ref = bf16[128,32,512]{2,1,0:T(8,128)(2,1)S(1)} all-to-all(bf16[128,32,512]{2,1,0:T(8,128)(2,1)S(1)} %bitcast.9), channel_id=1, replica_groups=mesh['dp'=16,'sub'=8] {'dp','sub'}, dimensions={0} | all-to-all | bytes 8388608 | tf_op jit(solution)/shard_map/all_to_all | solution.py:347
  72.2 4.7 %compare.1 = (f32[4,512]{1,0:T(4,128)}, f32[128,128]{1,0:T(8,128)S(1)}) custom-call(bf16[128,32,512]{2,1,0:T(8,128)(2,1)S(1)} %all_to_all.10.in_ref), custom_call_target="tpu_custom_call" | custom-call | tf_op jit(solution)/shard_map/compare/pallas_call | solution.py:271
  76.9 13.4 %all_to_all.11 = f32[128,1,128]{2,1,0:T(1,128)S(1)} all-to-all(f32[128,1,128]{2,1,0:T(1,128)S(1)} %bitcast.11), channel_id=1, replica_groups=mesh['dp'=16,'sub'=8] {'dp','sub'}, dimensions={0} | all-to-all | bytes 131072 | tf_op jit(solution)/shard_map/all_to_all | solution.py:351
  90.3 1.1 %pick.1 = (f32[1,2048]{1,0:T(1,128)}, f32[1,2048]{1,0:T(1,128)}) custom-call(f32[128,128]{1,0:T(8,128)S(1)} %bitcast.10, s32[1,2048]{1,0:T(1,128)S(1)} %get-tuple-element.12.flat_ref), custom_call_target="tpu_custom_call" | custom-call | tf_op jit(solution)/shard_map/pick/pallas_call | solution.py:328

commit v6 on v5

--- a/solution.py
+++ b/solution.py
@@ -181,7 +181,7 @@
 def compare_kernel(members, slot_size, in_ref, cent_ref, back_ref, held, pen, val_ref, turned):
     sources, slots, feats = in_ref.shape
     per_member = pen.shape[1]
-    batch = 8
+    batch = 16
     part = batch * slot_size
     cols = 256
     for pair in range(0, members, 2):

time: 91.6 us -> 91.7 us (level)
  no operation moved by 1% of the time
where the time goes in v6:
time: 91.7 us; the launch traced here: 91.5 us
  blocking collectives  77.7 us (85%)
  Pallas kernels  13.1 us (14%)
    all_to_all x1, blocking collectives, on_device(): lax.all_to_all(outgoing.reshape(devices, members * slot_size, feats), bot...  64.3 us
    all_to_all x1, blocking collectives, on_device(): lax.all_to_all(values.reshape(devices, 1, values.shape[1]), both, split_a...  13.4 us
    pallas_call x1, Pallas kernels, place(): pl.pallas_call(functools.partial(place_kernel, slot_size), in_specs=[hbm,...  7.28 us
    pallas_call x1, Pallas kernels, compare(): pl.pallas_call(functools.partial(compare_kernel, members, slot_size), in_...  4.69 us

profile of v6, /device:TPU:1, one launch (start us, length us, event | category | flops | bytes accessed | tf_op | source)
XLA Modules:
  0.0 91.5 jit_solution(8714340379508713562)
XLA Ops:
  0.6 7.3 %place.1 = (bf16[4096,512]{1,0:T(8,128)(2,1)S(1)}, s32[1,2048]{1,0:T(1,128)S(1)}) custom-call(s32[1,2048]{1,0:T(1,128)} %bitcast.12, s32[1,512]{1,0:T(1,128)} %bitcast.13, bf16[2048,512]{1,0:T(8,128)(2,1)} %emb_hbm.1), custom_call_target="tpu_custom_call" | custom-call | tf_op jit(solution)/shard_map/place/pallas_call | solution.py:158
  7.9 64.3 %all_to_all.10.in_ref = bf16[128,32,512]{2,1,0:T(8,128)(2,1)S(1)} all-to-all(bf16[128,32,512]{2,1,0:T(8,128)(2,1)S(1)} %bitcast.9), channel_id=1, replica_groups=mesh['dp'=16,'sub'=8] {'dp','sub'}, dimensions={0} | all-to-all | bytes 8388608 | tf_op jit(solution)/shard_map/all_to_all | solution.py:347
  72.2 4.7 %compare.1 = (f32[4,512]{1,0:T(4,128)}, f32[128,128]{1,0:T(8,128)S(1)}) custom-call(bf16[128,32,512]{2,1,0:T(8,128)(2,1)S(1)} %all_to_all.10.in_ref), custom_call_target="tpu_custom_call" | custom-call | tf_op jit(solution)/shard_map/compare/pallas_call | solution.py:271
  76.9 13.4 %all_to_all.11 = f32[128,1,128]{2,1,0:T(1,128)S(1)} all-to-all(f32[128,1,128]{2,1,0:T(1,128)S(1)} %bitcast.11), channel_id=1, replica_groups=mesh['dp'=16,'sub'=8] {'dp','sub'}, dimensions={0} | all-to-all | bytes 131072 | tf_op jit(solution)/shard_map/all_to_all | solution.py:351
  90.4 1.1 %pick.1 = (f32[1,2048]{1,0:T(1,128)}, f32[1,2048]{1,0:T(1,128)}) custom-call(f32[128,128]{1,0:T(8,128)S(1)} %bitcast.10, s32[1,2048]{1,0:T(1,128)S(1)} %get-tuple-element.12.flat_ref), custom_call_target="tpu_custom_call" | custom-call | tf_op jit(solution)/shard_map/pick/pallas_call | solution.py:328
